TPU v7x, 32 devices: a whole 2x2x4 slice. The times are simulated.
32 devices in a mesh: section: 2 (over y), expert: 16 (over z, x, core).
Axes of the slice: x: 2, y: 2, z: 4, core: 2. Of those that a mesh axis runs over, the one named last changes fastest.
Arguments:
- section_input: bfloat16 [2, 1536, 2048], P('section', 'expert'), may hold values from -6 to 6
- saved_input: bfloat16 [2, 1536, 2048], P('section', 'expert'), may hold values from -6 to 6
- grad_input: bfloat16 [2, 1536, 2048], P('section', 'expert'), may hold values from -6 to 6
- expert_ids: int32 [2, 2, 1536, 2], P('section', None, 'expert'), may hold values from 0 to 3, all different within a row; in each aligned block of 96 rows (0 to 95, 96 to 191, ..., all dimensions but the last counted through in order) at most 64 rows name the same one
- keep_mask: int32 [2, 2, 1536, 2], P('section', None, 'expert'), may hold values 0 or 1
- norm_gain: float32 [2, 2048], P('section'), may hold values from 0.5 to 1.5
- router_weight: bfloat16 [2, 2048, 4], P('section'), may hold values from -0.25 to 0.25
- gate_weight: bfloat16 [2, 2048, 3072], P('section', None, 'expert'), may hold values from -0.125 to 0.125
- up_weight: bfloat16 [2, 2048, 3072], P('section', None, 'expert'), may hold values from -0.125 to 0.125
- down_weight: bfloat16 [2, 3072, 2048], P('section', 'expert'), may hold values from -0.21875 to 0.21875
Outputs:
- section_output: bfloat16 [2, 1536, 2048], P('section', 'expert')
- grad_output: bfloat16 [2, 1536, 2048], P('section', 'expert')
Inputs may be any that keep to these rules, and one draw needn't show every extreme that they name: `expert_ids`: each token names 2 different experts. Among the 96 tokens that one index of expert holds for one section and micro-batch, no expert is named more than 64 times, a bound that some block reaches in some of them.
All inputs are finite; a program needn't handle non-finite values. No bound on the sum of `keep_mask` on one device may be relied on, other than what follows from the above.
Results may differ from a plain program's by a relative error of at most 0.012.
Values may be sent and summed in bfloat16 or wider, within the bound.
A program may use at most 64 MiB of HBM per device.

v0:
```python
import functools

import jax
import jax.numpy as jnp
from jax import lax
from jax.experimental import pallas as pl
from jax.experimental.pallas import tpu as pltpu
from jax.sharding import PartitionSpec as P

EPS = 1e-06
KEEP_SCALE = 8.0 / 7.0
MESH = pl.DeviceIdType.MESH
F32 = jnp.float32
BF16 = jnp.bfloat16


def rows_by_rows(left, right):
    return lax.dot_general(left, right, (((1,), (1,)), ((), ())), preferred_element_type=F32)


def matmul(left, right):
    return jnp.dot(left, right, preferred_element_type=F32)


def normalize(hidden, gain):
    plain = hidden.astype(F32)
    inverse = lax.rsqrt(jnp.mean(plain * plain, axis=-1, keepdims=True) + EPS)
    return inverse, (plain * inverse * gain).astype(BF16)


def routing(normed, router, ids, keep, capacity):
    tokens, experts = normed.shape[0], router.shape[1]
    top = ids.shape[1]
    logits = matmul(normed, router)
    lane = lax.broadcasted_iota(jnp.int32, (tokens, experts), 1)
    chosen = [ids[:, k : k + 1] == lane for k in range(top)]
    picked = [jnp.sum(jnp.where(c, logits, 0.0), axis=1, keepdims=True) for c in chosen]
    probs = []
    for k in range(top):
        spread = functools.reduce(jnp.add, [jnp.exp(p - picked[k]) for p in picked])
        probs.append(1.0 / spread)
    kept = [keep[:, k : k + 1].astype(F32) * KEEP_SCALE for k in range(top)]
    scale = [kept[k] * probs[k] for k in range(top)]
    named = functools.reduce(jnp.add, [jnp.where(c, 1.0, 0.0) for c in chosen])
    row = lax.broadcasted_iota(jnp.int32, (tokens, tokens), 0)
    column = lax.broadcasted_iota(jnp.int32, (tokens, tokens), 1)
    earlier = jnp.where(column < row, 1.0, 0.0).astype(BF16)
    rank = matmul(earlier, named.astype(BF16))
    place = lane.astype(F32) * capacity + rank
    slot = [jnp.sum(jnp.where(c, place, 0.0), axis=1, keepdims=True) for c in chosen]
    along = [jnp.sum(jnp.where(row == column, s, 0.0), axis=0, keepdims=True) for s in slot]
    table = lax.broadcasted_iota(jnp.int32, (experts * capacity, tokens), 0).astype(F32)
    fill = functools.reduce(jnp.add, [jnp.where(table == a, 1.0, 0.0) for a in along]).astype(BF16)
    return chosen, probs, kept, scale, slot, fill


def pickers(slot, slots):
    tokens = slot[0].shape[0]
    lane = lax.broadcasted_iota(jnp.int32, (tokens, slots), 1).astype(F32)
    return [jnp.where(lane == s, 1.0, 0.0).astype(BF16) for s in slot]


def layer(
    experts,
    replicas,
    sections,
    capacity,
    fwd_in,
    bwd_in,
    grad_in,
    ids_ref,
    keep_ref,
    gain_ref,
    router_ref,
    gate_ref,
    up_ref,
    down_ref,
    fwd_out,
    bwd_out,
    w_gate,
    w_up,
    w_down,
    sent,
    got,
    done,
    back,
    change_done,
    change_back,
    inner,
    grad_gate,
    grad_up,
    weighted,
    staged,
    quarter_send,
    quarter_recv,
    row_send,
    row_recv,
    back_send,
    back_recv,
    hand_send,
    hand_recv,
):
    section = lax.axis_index("section")
    me = lax.axis_index("expert")
    group, replica = me // replicas, me % replicas
    tokens, width = fwd_in.shape
    quarter = down_ref.shape[0]
    hidden = quarter * replicas
    slots = experts * capacity
    core_mate = group * replicas + (replica + 1 - 2 * (replica % 2))
    chip_mate = group * replicas + (replica + 2) % replicas
    following = (section + 1) % sections
    previous = (section + sections - 1) % sections

    barrier = pltpu.get_barrier_semaphore()
    mates = [{"expert": core_mate}, {"expert": chip_mate}]
    mates += [{"section": following}, {"section": previous}]
    others = [(group + d) % experts for d in range(1, experts)]
    mates += [{"expert": other * replicas + replica} for other in others]
    for mate in mates:
        pl.semaphore_signal(barrier, inc=1, device_id=mate, device_id_type=MESH)
    pl.semaphore_wait(barrier, len(mates))

    weights = [w_down, w_gate, w_up]
    started = []

    def quarter_copy(which, place, mate, source):
        copy = pltpu.make_async_remote_copy(
            src_ref=source,
            dst_ref=weights[which].at[pl.ds(place * quarter, quarter)],
            send_sem=quarter_send.at[place, which],
            recv_sem=quarter_recv.at[place, which],
            device_id={"expert": mate},
            device_id_type=MESH,
        )
        copy.start()
        started.append(copy)
        return copy

    def row_block(ref, index):
        return ref.at[pl.ds(pl.multiple_of(index * capacity, capacity), capacity)]

    def trade(source, target, send_sem, recv_sem):
        copies = []
        for place, other in enumerate(others):
            copy = pltpu.make_async_remote_copy(
                src_ref=row_block(source, other),
                dst_ref=row_block(target, group),
                send_sem=send_sem.at[place],
                recv_sem=recv_sem.at[place],
                device_id={"expert": other * replicas + replica},
                device_id_type=MESH,
            )
            copy.start()
            copies.append(copy)
        started.extend(copies)
        own = pl.ds(pl.multiple_of(group * capacity, capacity), capacity)
        target[own, :] = source[own, :]
        return copies

    across = [quarter_copy(0, 2, chip_mate, down_ref)]
    quarter_copy(0, 1, core_mate, down_ref)

    gain = gain_ref[...]
    router = router_ref[...]
    fwd_inverse, fwd_normed = normalize(fwd_in[...], gain)
    del fwd_inverse
    fwd_route = routing(fwd_normed, router, ids_ref[0], keep_ref[0], capacity)
    sent[0] = matmul(fwd_route[5], fwd_normed).astype(BF16)
    moves = [trade(sent.at[0], got.at[0], row_send.at[0], row_recv.at[0])]

    eye = jnp.where(
        lax.broadcasted_iota(jnp.int32, (quarter, quarter), 0)
        == lax.broadcasted_iota(jnp.int32, (quarter, quarter), 1),
        1.0,
        0.0,
    ).astype(BF16)
    for which, source, target in ((1, gate_ref, w_gate), (2, up_ref, w_up)):
        target[0:quarter, :] = rows_by_rows(eye, source[...]).astype(BF16)
        own_piece = target.at[pl.ds(0, quarter)]
        across.append(quarter_copy(which, 2, chip_mate, own_piece))
        quarter_copy(which, 1, core_mate, own_piece)
    w_down[0:quarter, :] = down_ref[...]

    bwd_inverse, bwd_normed = normalize(bwd_in[...], gain)
    bwd_route = routing(bwd_normed, router, ids_ref[1], keep_ref[1], capacity)
    sent[1] = matmul(bwd_route[5], bwd_normed).astype(BF16)
    moves.append(trade(sent.at[1], got.at[1], row_send.at[1], row_recv.at[1]))
    sent[2] = matmul(bwd_route[5], grad_in[...]).astype(BF16)
    moves.append(trade(sent.at[2], got.at[2], row_send.at[2], row_recv.at[2]))

    for which, copy in enumerate(across):
        copy.wait_recv()
        quarter_copy(which, 3, core_mate, weights[which].at[pl.ds(2 * quarter, quarter)])
    for place in (1, 3):
        for which in range(3):
            pltpu.make_async_remote_copy(
                src_ref=down_ref,
                dst_ref=weights[which].at[pl.ds(place * quarter, quarter)],
                send_sem=quarter_send.at[place, which],
                recv_sem=quarter_recv.at[place, which],
                device_id={"expert": core_mate},
                device_id_type=MESH,
            ).wait_recv()

    step = 256 if hidden % 256 == 0 else quarter
    wide = 512 if width % 512 == 0 else width

    def part(index, size):
        return pl.ds(pl.multiple_of(index * size, size), size)

    for copy in moves[0]:
        copy.wait_recv()

    @pl.loop(0, hidden // step)
    def _(h):
        rows = got[0]
        pre_gate = rows_by_rows(rows, w_gate[part(h, step), :])
        pre_up = rows_by_rows(rows, w_up[part(h, step), :])
        inner[:, part(h, step)] = (pre_gate * jax.nn.sigmoid(pre_gate) * pre_up).astype(BF16)

    @pl.loop(0, width // wide)
    def _(c):
        done[0, :, part(c, wide)] = matmul(inner[...], w_down[:, part(c, wide)]).astype(BF16)

    returns = [trade(done.at[0], back.at[0], back_send.at[0], back_recv.at[0])]

    for copy in moves[1] + moves[2]:
        copy.wait_recv()

    def backward_step(h, change):
        rows = got[1]
        pre_gate = rows_by_rows(rows, w_gate[part(h, step), :])
        pre_up = rows_by_rows(rows, w_up[part(h, step), :])
        pulled = rows_by_rows(got[2], w_down[part(h, step), :])
        sigma = jax.nn.sigmoid(pre_gate)
        act = (pre_gate * sigma * pre_up).astype(BF16).astype(F32)
        grad_gate[:, part(h, step)] = (
            pulled * pre_up * sigma * (1.0 + pre_gate * (1.0 - sigma))
        ).astype(BF16)
        grad_up[:, part(h, step)] = (pulled * pre_gate * sigma).astype(BF16)
        return change + jnp.sum(act * pulled, axis=1, keepdims=True)

    change = lax.fori_loop(0, hidden // step, backward_step, jnp.zeros((slots, 1), F32))
    change_done[...] = jnp.broadcast_to(change, change_done.shape).astype(BF16)
    change_moves = trade(change_done, change_back, back_send.at[2], back_recv.at[2])

    @pl.loop(0, width // wide)
    def _(c):
        total = matmul(grad_gate[...], w_gate[:, part(c, wide)])
        total += matmul(grad_up[...], w_up[:, part(c, wide)])
        done[1, :, part(c, wide)] = total.astype(BF16)

    returns.append(trade(done.at[1], back.at[1], back_send.at[1], back_recv.at[1]))

    for copy in returns[0]:
        copy.wait_recv()
    fwd_pick = pickers(fwd_route[4], slots)
    fwd_scale = fwd_route[3]

    @pl.loop(0, width // wide)
    def _(c):
        total = fwd_in[:, part(c, wide)].astype(F32)
        mixed = None
        for pick, scale in zip(fwd_pick, fwd_scale):
            term = scale * matmul(pick, back[0, :, part(c, wide)])
            mixed = term if mixed is None else mixed + term
        staged[0, :, part(c, wide)] = (total + mixed).astype(BF16)

    hand_fwd = pltpu.make_async_remote_copy(
        src_ref=staged.at[0],
        dst_ref=fwd_out.at[0],
        send_sem=hand_send.at[0],
        recv_sem=hand_recv.at[0],
        device_id={"section": following},
        device_id_type=MESH,
    )
    hand_fwd.start()

    for copy in change_moves + returns[1]:
        copy.wait_recv()
    chosen, probs, kept, scale, slot, _ = bwd_route
    pick = pickers(slot, slots)
    moved = [kept[k] * matmul(pick[k], change_back[...])[:, 0:1] for k in range(len(pick))]
    balance = functools.reduce(jnp.add, [probs[k] * moved[k] for k in range(len(pick))])
    logit_grad = [probs[k] * (moved[k] - balance) for k in range(len(pick))]
    dense = functools.reduce(
        jnp.add, [jnp.where(chosen[k], logit_grad[k], 0.0) for k in range(len(pick))]
    )
    dense_high = dense.astype(BF16)
    dense_low = (dense - dense_high.astype(F32)).astype(BF16)

    def gather_step(c, dots):
        total = None
        for k in range(len(pick)):
            term = scale[k] * matmul(pick[k], back[1, :, part(c, wide)])
            total = term if total is None else total + term
        near_router = router_ref[part(c, wide), :]
        total += rows_by_rows(dense_high, near_router) + rows_by_rows(dense_low, near_router)
        gained = total * gain_ref[:, part(c, wide)]
        weighted[:, part(c, wide)] = gained
        plain = bwd_in[:, part(c, wide)].astype(F32)
        return dots + jnp.sum(gained * plain, axis=1, keepdims=True)

    dots = lax.fori_loop(0, width // wide, gather_step, jnp.zeros((tokens, 1), F32))
    factor = bwd_inverse * bwd_inverse * (dots * (1.0 / width))

    @pl.loop(0, width // wide)
    def _(c):
        plain = bwd_in[:, part(c, wide)].astype(F32)
        norm_grad = bwd_inverse * (weighted[:, part(c, wide)] - plain * factor)
        staged[1, :, part(c, wide)] = (grad_in[:, part(c, wide)].astype(F32) + norm_grad).astype(
            BF16
        )

    hand_bwd = pltpu.make_async_remote_copy(
        src_ref=staged.at[1],
        dst_ref=bwd_out.at[0],
        send_sem=hand_send.at[1],
        recv_sem=hand_recv.at[1],
        device_id={"section": previous},
        device_id_type=MESH,
    )
    hand_bwd.start()
    for copy in started:
        copy.wait_send()
    hand_fwd.wait()
    hand_bwd.wait()


def on_device(
    section_input,
    saved_input,
    grad_input,
    expert_ids,
    keep_mask,
    norm_gain,
    router_weight,
    gate_weight,
    up_weight,
    down_weight,
):
    tokens, width = section_input.shape[1:]
    experts = router_weight.shape[2]
    top = expert_ids.shape[3]
    replicas = lax.axis_size("expert") // experts
    sections = lax.axis_size("section")
    capacity = 4 * tokens * top // (3 * experts)
    slots = experts * capacity
    quarter = down_weight.shape[1]
    hidden = quarter * replicas
    dma = pltpu.SemaphoreType.DMA
    vmem = pl.BlockSpec(memory_space=pltpu.VMEM)
    result = jax.ShapeDtypeStruct((1, tokens, width), BF16)
    return pl.pallas_call(
        functools.partial(layer, experts, replicas, sections, capacity),
        out_shape=(result, result),
        in_specs=[vmem] * 10,
        out_specs=(pl.BlockSpec(memory_space=pl.ANY),) * 2,
        scratch_shapes=[
            pltpu.VMEM((hidden, width), BF16),
            pltpu.VMEM((hidden, width), BF16),
            pltpu.VMEM((hidden, width), BF16),
            pltpu.VMEM((3, slots, width), BF16),
            pltpu.VMEM((3, slots, width), BF16),
            pltpu.VMEM((2, slots, width), BF16),
            pltpu.VMEM((2, slots, width), BF16),
            pltpu.VMEM((slots, 128), BF16),
            pltpu.VMEM((slots, 128), BF16),
            pltpu.VMEM((slots, hidden), BF16),
            pltpu.VMEM((slots, hidden), BF16),
            pltpu.VMEM((slots, hidden), BF16),
            pltpu.VMEM((tokens, width), F32),
            pltpu.VMEM((2, tokens, width), BF16),
            dma((4, 3)),
            dma((4, 3)),
            dma((3, experts - 1)),
            dma((3, experts - 1)),
            dma((3, experts - 1)),
            dma((3, experts - 1)),
            dma((2,)),
            dma((2,)),
        ],
        compiler_params=pltpu.CompilerParams(
            collective_id=0, has_side_effects=True, vmem_limit_bytes=56 * 1024 * 1024
        ),
    )(
        section_input[0],
        saved_input[0],
        grad_input[0],
        expert_ids[0],
        keep_mask[0],
        norm_gain,
        router_weight[0],
        gate_weight[0],
        up_weight[0],
        down_weight[0],
    )


def solution(mesh):
    return jax.shard_map(
        on_device,
        mesh=mesh,
        in_specs=(
            P("section", "expert", None),
            P("section", "expert", None),
            P("section", "expert", None),
            P("section", None, "expert", None),
            P("section", None, "expert", None),
            P("section", None),
            P("section", None, None),
            P("section", None, "expert"),
            P("section", None, "expert"),
            P("section", "expert", None),
        ),
        out_specs=(P("section", "expert", None), P("section", "expert", None)),
        check_vma=False,
    )
```

profile of v0, /device:TPU:10, one launch (start us, length us, event | category | flops | bytes accessed | tf_op | source)
XLA Modules:
  0.0 144.2 jit_solution(767496649623074495)
XLA Ops:
  0.6 0.0 copy-start.3
  0.6 0.7 copy-done.3
  1.3 0.0 copy-start.4
  1.3 0.8 copy.12
  2.1 0.0 copy-done.4
  2.1 0.0 copy-start.2
  2.1 0.8 copy.13
  2.9 0.0 copy-done.2
  2.9 1.1 copy.14
  3.9 0.0 copy-start
  3.9 2.3 %copy.15 = bf16[1,2048,192]{2,1,0:T(8,128)(2,1)} copy(bf16[1,2048,192]{1,2,0:T(8,128)(2,1)} %param.17) | data formatting | bytes 1572864 | tf_op args[7]
  6.2 0.0 copy-done
  6.2 1.3 copy.16
  7.5 134.1 %shard_map.113 = (bf16[1,96,2048]{2,1,0:T(8,128)(2,1)}, bf16[1,96,2048]{2,1,0:T(8,128)(2,1)}) custom-call(bf16[96,2048]{1,0:T(8,128)(2,1)} %bitcast.13, bf16[96,2048]{1,0:T(8,128)(2,1)} %bitcast.14, bf16[96,2048]{1,0:T(8,128)(2,1)} %bitcast.15, s32[2,96,2]{2,1,0:T(8,128)} %bitcast.16, s32[2,96,2]{2,1,0:T(8,128)} %bitcast.17, f32[1,2048]{1,0:T(1,128)} %gain_ref.1, ...), custom_call_target="tpu_custom_call" | custom-call | tf_op jit(solution)/shard_map/pallas_call | solution.py:355
  141.6 0.0 copy-start.1
  141.6 1.8 %copy.19 = bf16[1,96,2048]{2,1,0:T(8,128)(2,1)} copy(bf16[1,96,2048]{2,1,0:T(8,128)(2,1)} %get-tuple-element.4) | data formatting | bytes 786432
  143.4 0.0 copy-done.1
  143.4 0.7 copy.20
Async XLA Ops:
  0.6 0.7 copy-start.3
  1.3 0.8 copy-start.4
  2.1 0.8 copy-start.2
  3.9 2.3 %copy-start = (bf16[1,2048,192]{1,2,0:T(8,128)(2,1)S(1)}, bf16[1,2048,192]{1,2,0:T(8,128)(2,1)}, u32[]{:S(2)}) copy-start(bf16[1,2048,192]{1,2,0:T(8,128)(2,1)} %param.18) | copy-start | bytes 2359300
  141.6 1.8 %copy-start.1 = (bf16[1,96,2048]{2,1,0:T(8,128)(2,1)S(1)}, bf16[1,96,2048]{2,1,0:T(8,128)(2,1)}, u32[]{:S(2)}) copy-start(bf16[1,96,2048]{2,1,0:T(8,128)(2,1)} %get-tuple-element.5) | copy-start | bytes 1179652
where the time goes:
time: 144 us
  Pallas kernels  134 us (93%)
  local copies, waits for them, and re-layouts  9.43 us (7%)
    pallas_call x1, Pallas kernels, on_device(): pl.pallas_call(functools.partial(layer, experts, replicas, sections, capa...  134 us
    unnamed x17, local copies, waits for them, and re-layouts  9.43 us

commit v1 on v0

--- a/solution.py
+++ b/solution.py
@@ -28,22 +28,28 @@
     return inverse, (plain * inverse * gain).astype(BF16)
 
 
-def routing(normed, router, ids, keep, capacity):
-    tokens, experts = normed.shape[0], router.shape[1]
-    top = ids.shape[1]
-    logits = matmul(normed, router)
+def routing(normed, router, id_rows, keep_rows, capacity):
+    tokens, experts = normed.shape[0], router.shape[0]
+    top = id_rows.shape[0]
+    logits = rows_by_rows(normed, router)
     lane = lax.broadcasted_iota(jnp.int32, (tokens, experts), 1)
-    chosen = [ids[:, k : k + 1] == lane for k in range(top)]
+    row = lax.broadcasted_iota(jnp.int32, (tokens, tokens), 0)
+    column = lax.broadcasted_iota(jnp.int32, (tokens, tokens), 1)
+
+    def upright(line):
+        spread_out = jnp.where(row == column, line.astype(F32), 0.0)
+        return jnp.sum(spread_out, axis=1, keepdims=True)
+
+    ids = [upright(id_rows[k : k + 1, :]) for k in range(top)]
+    chosen = [i == lane.astype(F32) for i in ids]
     picked = [jnp.sum(jnp.where(c, logits, 0.0), axis=1, keepdims=True) for c in chosen]
     probs = []
     for k in range(top):
         spread = functools.reduce(jnp.add, [jnp.exp(p - picked[k]) for p in picked])
         probs.append(1.0 / spread)
-    kept = [keep[:, k : k + 1].astype(F32) * KEEP_SCALE for k in range(top)]
+    kept = [upright(keep_rows[k : k + 1, :]) * KEEP_SCALE for k in range(top)]
     scale = [kept[k] * probs[k] for k in range(top)]
     named = functools.reduce(jnp.add, [jnp.where(c, 1.0, 0.0) for c in chosen])
-    row = lax.broadcasted_iota(jnp.int32, (tokens, tokens), 0)
-    column = lax.broadcasted_iota(jnp.int32, (tokens, tokens), 1)
     earlier = jnp.where(column < row, 1.0, 0.0).astype(BF16)
     rank = matmul(earlier, named.astype(BF16))
     place = lane.astype(F32) * capacity + rank
@@ -158,8 +164,10 @@
         target[own, :] = source[own, :]
         return copies
 
-    across = [quarter_copy(0, 2, chip_mate, down_ref)]
-    quarter_copy(0, 1, core_mate, down_ref)
+    across = []
+    for which, source in enumerate((down_ref, gate_ref, up_ref)):
+        across.append(quarter_copy(which, 2, chip_mate, source))
+        quarter_copy(which, 1, core_mate, source)
 
     gain = gain_ref[...]
     router = router_ref[...]
@@ -169,19 +177,6 @@
     sent[0] = matmul(fwd_route[5], fwd_normed).astype(BF16)
     moves = [trade(sent.at[0], got.at[0], row_send.at[0], row_recv.at[0])]
 
-    eye = jnp.where(
-        lax.broadcasted_iota(jnp.int32, (quarter, quarter), 0)
-        == lax.broadcasted_iota(jnp.int32, (quarter, quarter), 1),
-        1.0,
-        0.0,
-    ).astype(BF16)
-    for which, source, target in ((1, gate_ref, w_gate), (2, up_ref, w_up)):
-        target[0:quarter, :] = rows_by_rows(eye, source[...]).astype(BF16)
-        own_piece = target.at[pl.ds(0, quarter)]
-        across.append(quarter_copy(which, 2, chip_mate, own_piece))
-        quarter_copy(which, 1, core_mate, own_piece)
-    w_down[0:quarter, :] = down_ref[...]
-
     bwd_inverse, bwd_normed = normalize(bwd_in[...], gain)
     bwd_route = routing(bwd_normed, router, ids_ref[1], keep_ref[1], capacity)
     sent[1] = matmul(bwd_route[5], bwd_normed).astype(BF16)
@@ -189,6 +184,8 @@
     sent[2] = matmul(bwd_route[5], grad_in[...]).astype(BF16)
     moves.append(trade(sent.at[2], got.at[2], row_send.at[2], row_recv.at[2]))
 
+    for target, source in zip(weights, (down_ref, gate_ref, up_ref)):
+        target[0:quarter, :] = source[...]
     for which, copy in enumerate(across):
         copy.wait_recv()
         quarter_copy(which, 3, core_mate, weights[which].at[pl.ds(2 * quarter, quarter)])
@@ -290,42 +287,43 @@
     dense_high = dense.astype(BF16)
     dense_low = (dense - dense_high.astype(F32)).astype(BF16)
 
-    def gather_step(c, dots):
-        total = None
-        for k in range(len(pick)):
-            term = scale[k] * matmul(pick[k], back[1, :, part(c, wide)])
-            total = term if total is None else total + term
-        near_router = router_ref[part(c, wide), :]
-        total += rows_by_rows(dense_high, near_router) + rows_by_rows(dense_low, near_router)
-        gained = total * gain_ref[:, part(c, wide)]
-        weighted[:, part(c, wide)] = gained
-        plain = bwd_in[:, part(c, wide)].astype(F32)
-        return dots + jnp.sum(gained * plain, axis=1, keepdims=True)
-
-    dots = lax.fori_loop(0, width // wide, gather_step, jnp.zeros((tokens, 1), F32))
-    factor = bwd_inverse * bwd_inverse * (dots * (1.0 / width))
-
-    @pl.loop(0, width // wide)
-    def _(c):
-        plain = bwd_in[:, part(c, wide)].astype(F32)
-        norm_grad = bwd_inverse * (weighted[:, part(c, wide)] - plain * factor)
-        staged[1, :, part(c, wide)] = (grad_in[:, part(c, wide)].astype(F32) + norm_grad).astype(
-            BF16
+    span = 32 if tokens % 32 == 0 else tokens
+    hand_bwd = []
+    for piece in range(tokens // span):
+        own = slice(piece * span, (piece + 1) * span)
+
+        def gather_step(c, dots):
+            total = None
+            for k in range(len(pick)):
+                term = scale[k][own] * matmul(pick[k][own], back[1, :, part(c, wide)])
+                total = term if total is None else total + term
+            near_router = router_ref[:, part(c, wide)]
+            total += matmul(dense_high[own], near_router) + matmul(dense_low[own], near_router)
+            gained = total * gain_ref[:, part(c, wide)]
+            weighted[own, part(c, wide)] = gained
+            plain = bwd_in[own, part(c, wide)].astype(F32)
+            return dots + jnp.sum(gained * plain, axis=1, keepdims=True)
+
+        dots = lax.fori_loop(0, width // wide, gather_step, jnp.zeros((span, 1), F32))
+        inverse = bwd_inverse[own]
+        factor = inverse * inverse * (dots * (1.0 / width))
+        norm_grad = inverse * (weighted[own, :] - bwd_in[own, :].astype(F32) * factor)
+        staged[1, own, :] = (grad_in[own, :].astype(F32) + norm_grad).astype(BF16)
+        copy = pltpu.make_async_remote_copy(
+            src_ref=staged.at[1, pl.ds(piece * span, span)],
+            dst_ref=bwd_out.at[0, pl.ds(piece * span, span)],
+            send_sem=hand_send.at[1 + piece],
+            recv_sem=hand_recv.at[1 + piece],
+            device_id={"section": previous},
+            device_id_type=MESH,
         )
-
-    hand_bwd = pltpu.make_async_remote_copy(
-        src_ref=staged.at[1],
-        dst_ref=bwd_out.at[0],
-        send_sem=hand_send.at[1],
-        recv_sem=hand_recv.at[1],
-        device_id={"section": previous},
-        device_id_type=MESH,
-    )
-    hand_bwd.start()
+        copy.start()
+        hand_bwd.append(copy)
     for copy in started:
         copy.wait_send()
     hand_fwd.wait()
-    hand_bwd.wait()
+    for copy in hand_bwd:
+        copy.wait()
 
 
 def on_device(
@@ -378,8 +376,8 @@
             dma((3, experts - 1)),
             dma((3, experts - 1)),
             dma((3, experts - 1)),
-            dma((2,)),
-            dma((2,)),
+            dma((1 + tokens // 32,)),
+            dma((1 + tokens // 32,)),
         ],
         compiler_params=pltpu.CompilerParams(
             collective_id=0, has_side_effects=True, vmem_limit_bytes=56 * 1024 * 1024
@@ -388,12 +386,12 @@
         section_input[0],
         saved_input[0],
         grad_input[0],
-        expert_ids[0],
-        keep_mask[0],
+        jnp.swapaxes(expert_ids[0], 1, 2),
+        jnp.swapaxes(keep_mask[0], 1, 2),
         norm_gain,
-        router_weight[0],
-        gate_weight[0],
-        up_weight[0],
+        router_weight[0].T,
+        gate_weight[0].T,
+        up_weight[0].T,
         down_weight[0],
     )
 

time: 144 us -> 136 us (0.944)
  local copies, waits for them, and re-layouts: 9.43 us -> 2.57 us
    unnamed x17 -> x4, local copies, waits for them, and re-layouts: 9.43 us -> 2.57 us
where the time goes in v1:
time: 136 us
  Pallas kernels  133 us (98%)
  local copies, waits for them, and re-layouts  2.57 us (2%)
    pallas_call x1, Pallas kernels, on_device(): pl.pallas_call(functools.partial(layer, experts, replicas, sections, capa...  133 us

profile of v1, /device:TPU:10, one launch (start us, length us, event | category | flops | bytes accessed | tf_op | source)
XLA Modules:
  0.0 136.2 jit_solution(10305364516970957024)
XLA Ops:
  0.6 133.0 %shard_map.113 = (bf16[1,96,2048]{2,1,0:T(8,128)(2,1)}, bf16[1,96,2048]{2,1,0:T(8,128)(2,1)}) custom-call(bf16[96,2048]{1,0:T(8,128)(2,1)} %bitcast.22, bf16[96,2048]{1,0:T(8,128)(2,1)} %bitcast.23, bf16[96,2048]{1,0:T(8,128)(2,1)} %bitcast.24, s32[2,2,96]{2,1,0:T(2,128)} %bitcast.26, s32[2,2,96]{2,1,0:T(2,128)} %bitcast.27, f32[1,2048]{1,0:T(1,128)} %gain_ref.1, ...), custom_call_target="tpu_custom_call" | custom-call | tf_op jit(solution)/shard_map/pallas_call | solution.py:353
  133.6 0.0 copy-start
  133.6 1.8 %copy.14 = bf16[1,96,2048]{2,1,0:T(8,128)(2,1)} copy(bf16[1,96,2048]{2,1,0:T(8,128)(2,1)} %get-tuple-element.4) | data formatting | bytes 786432
  135.4 0.0 copy-done
  135.4 0.7 copy.15
Async XLA Ops:
  133.6 1.8 %copy-start = (bf16[1,96,2048]{2,1,0:T(8,128)(2,1)S(1)}, bf16[1,96,2048]{2,1,0:T(8,128)(2,1)}, u32[]{:S(2)}) copy-start(bf16[1,96,2048]{2,1,0:T(8,128)(2,1)} %get-tuple-element.5) | copy-start | bytes 1179652

commit v2 on v1

--- a/solution.py
+++ b/solution.py
@@ -242,13 +242,24 @@
     change_done[...] = jnp.broadcast_to(change, change_done.shape).astype(BF16)
     change_moves = trade(change_done, change_back, back_send.at[2], back_recv.at[2])
 
-    @pl.loop(0, width // wide)
-    def _(c):
-        total = matmul(grad_gate[...], w_gate[:, part(c, wide)])
-        total += matmul(grad_up[...], w_up[:, part(c, wide)])
-        done[1, :, part(c, wide)] = total.astype(BF16)
-
-    returns.append(trade(done.at[1], back.at[1], back_send.at[1], back_recv.at[1]))
+    half = width // 2
+    sides = []
+    for side in range(2):
+
+        @pl.loop(side * (half // wide), (side + 1) * (half // wide))
+        def _(c):
+            total = matmul(grad_gate[...], w_gate[:, part(c, wide)])
+            total += matmul(grad_up[...], w_up[:, part(c, wide)])
+            done[1, :, part(c, wide)] = total.astype(BF16)
+
+        columns = pl.ds(side * half, half)
+        sides += trade(
+            done.at[1, :, columns],
+            back.at[1, :, columns],
+            back_send.at[1 + 2 * side],
+            back_recv.at[1 + 2 * side],
+        )
+    returns.append(sides)
 
     for copy in returns[0]:
         copy.wait_recv()
@@ -374,8 +385,8 @@
             dma((4, 3)),
             dma((3, experts - 1)),
             dma((3, experts - 1)),
-            dma((3, experts - 1)),
-            dma((3, experts - 1)),
+            dma((4, experts - 1)),
+            dma((4, experts - 1)),
             dma((1 + tokens // 32,)),
             dma((1 + tokens // 32,)),
         ],

time: 136 us -> 136 us (level)
  no operation moved by 1% of the time
where the time goes in v2:
time: 136 us
  Pallas kernels  133 us (98%)
  local copies, waits for them, and re-layouts  2.57 us (2%)
    pallas_call x1, Pallas kernels, on_device(): pl.pallas_call(functools.partial(layer, experts, replicas, sections, capa...  133 us

profile of v2, /device:TPU:10, one launch (start us, length us, event | category | flops | bytes accessed | tf_op | source)
XLA Modules:
  0.0 136.2 jit_solution(4207516162196632052)
XLA Ops:
  0.6 133.0 %shard_map.113 = (bf16[1,96,2048]{2,1,0:T(8,128)(2,1)}, bf16[1,96,2048]{2,1,0:T(8,128)(2,1)}) custom-call(bf16[96,2048]{1,0:T(8,128)(2,1)} %bitcast.22, bf16[96,2048]{1,0:T(8,128)(2,1)} %bitcast.23, bf16[96,2048]{1,0:T(8,128)(2,1)} %bitcast.24, s32[2,2,96]{2,1,0:T(2,128)} %bitcast.26, s32[2,2,96]{2,1,0:T(2,128)} %bitcast.27, f32[1,2048]{1,0:T(1,128)} %gain_ref.1, ...), custom_call_target="tpu_custom_call" | custom-call | tf_op jit(solution)/shard_map/pallas_call | solution.py:364
  133.7 0.0 copy-start
  133.7 1.8 %copy.14 = bf16[1,96,2048]{2,1,0:T(8,128)(2,1)} copy(bf16[1,96,2048]{2,1,0:T(8,128)(2,1)} %get-tuple-element.4) | data formatting | bytes 786432
  135.5 0.0 copy-done
  135.5 0.7 copy.15
Async XLA Ops:
  133.7 1.8 %copy-start = (bf16[1,96,2048]{2,1,0:T(8,128)(2,1)S(1)}, bf16[1,96,2048]{2,1,0:T(8,128)(2,1)}, u32[]{:S(2)}) copy-start(bf16[1,96,2048]{2,1,0:T(8,128)(2,1)} %get-tuple-element.5) | copy-start | bytes 1179652
